TPU v7x, 1024 devices: a whole 4x4x32 slice. The times are simulated.
1024 devices in a mesh: dp: 32 (over z_hi, y, core), seq: 32 (over z_lo, x).
Axes of the slice: x: 4, y: 4, z: 32 (z_hi: 4, z_lo: 8; z = z_hi * 8 + z_lo), core: 2. Of those that a mesh axis runs over, the one named last changes fastest.
Arguments:
- queries: bfloat16 [32, 4096, 4096], P('dp', 'seq'), may hold values from -150 to 150
- keys: bfloat16 [32, 4096, 512], P('dp', 'seq'), may hold values from -6 to 6
- values: bfloat16 [32, 4096, 512], P('dp', 'seq'), may hold values from -6 to 6
- grad_out: bfloat16 [32, 4096, 4096], P('dp', 'seq'), may hold values from -6 to 6
- proj_in: bfloat16 [32, 4096, 256], P('dp', 'seq'), may hold values from -6 to 6
- segments: int32 [32, 4096], P('dp'), may hold values from 0 to 63, never falling along the last dimension, each value on 1 to 128 neighbouring positions
Outputs:
- grad_q_proj: float32 [256, 4096], P('dp', 'seq')
- grad_kv_proj: float32 [256, 1024], P('dp', 'seq')
Inputs may be any that keep to these rules, and one draw needn't show every extreme that they name: `segments`: document numbers never fall along a sequence; each document has 1 to 128 tokens, and some document has exactly 128.
All inputs are finite; a program needn't handle non-finite values.
Results may differ from a plain program's by a relative error of at most 0.025.
Values may be sent and summed in bfloat16 or wider, within the bound.
A program may use at most 64 MiB of HBM per device.

v0:
```python
import jax
import jax.numpy as jnp
from jax import lax
from jax.sharding import PartitionSpec as P

H = 32
KV = 4
HD = 128
RANK = 256
DOC = 128


def side_by_side(arrays, axis, split_dim, concat_dim, along):
    widths = [a.shape[along] for a in arrays]
    both = jnp.concatenate(arrays, axis=along)
    whole = lax.all_to_all(both, axis, split_axis=split_dim, concat_axis=concat_dim, tiled=True)
    return tuple(jnp.split(whole, [sum(widths[:k]) for k in range(1, len(widths))], axis=along))


def cut_along(value, dim, size):
    dims = value.shape
    tiles = value.reshape(*dims[:dim], size, dims[dim] // size, *dims[dim + 1 :])
    return jnp.moveaxis(tiles, dim, 0)


def summed_on_arrival(value, axis, dim):
    size = lax.axis_size(axis)
    tiles = lax.all_to_all(cut_along(value, dim, size), axis, 0, 0, tiled=True)
    return jnp.sum(tiles.astype(jnp.float32), axis=0)


def sum_packed(arrays, axis, dims):
    size = lax.axis_size(axis)
    tiles = [cut_along(a, dim, size) for a, dim in zip(arrays, dims)]
    lines = jnp.concatenate([b.reshape(size, -1) for b in tiles], axis=1)
    rows = max(16, -(-lines.shape[1] // 1024) * 8)
    lines = jnp.pad(lines, ((0, 0), (0, rows * 128 - lines.shape[1]))).reshape(-1, 128)
    flat, at, gathered = (lax.psum_scatter(lines, axis, tiled=True).reshape(-1), 0, [])
    for b in tiles:
        part = b[0]
        gathered.append(flat[at : at + part.size].reshape(part.shape))
        at += part.size
    return tuple(gathered)


def shifted_window(blocks, filler):
    previous = jnp.concatenate([jnp.full_like(blocks[:1], filler), blocks[:-1]], axis=0)
    return jnp.concatenate([previous, blocks], axis=1)


def attend(q_heads, k_heads, v_heads, g_heads, segment):
    length = q_heads.shape[0]
    head_count = q_heads.shape[1]
    head_width = q_heads.shape[2]
    block_count = length // DOC
    group_size = min(512 // DOC, block_count)
    scaling = head_width ** (-0.5)

    def to_blocks(array):
        return array.reshape((block_count, DOC) + array.shape[1:])

    def grouped(array):
        return array.reshape((block_count // group_size, group_size) + array.shape[1:])

    seg_query = to_blocks(segment)
    seg_key = shifted_window(seg_query, -1)
    q_block = to_blocks(q_heads)
    g_block = to_blocks(g_heads)
    k_window = shifted_window(to_blocks(k_heads), 0.0)
    v_window = shifted_window(to_blocks(v_heads), 0.0)
    causal = jnp.arange(2 * DOC)[None, :] <= jnp.arange(DOC)[:, None] + DOC

    def one_group(items):
        q_part, g_part, k_part, v_part, sq_part, sk_part = items
        allowed = (sq_part[:, :, None] == sk_part[:, None, :]) & causal[None]
        allowed = allowed[:, None]
        scores = (
            jnp.einsum("nqhd,nkhd->nhqk", q_part, k_part, preferred_element_type=jnp.float32)
            * scaling
        )
        scores = jnp.where(allowed, scores, -1e30)
        probs = jnp.exp(scores - jnp.max(scores, axis=-1, keepdims=True))
        probs = jnp.where(allowed, probs, 0.0)
        probs = probs / jnp.sum(probs, axis=-1, keepdims=True)
        probs_b = probs.astype(jnp.bfloat16)
        attn_out = jnp.einsum(
            "nhqk,nkhd->nqhd", probs_b, v_part, preferred_element_type=jnp.float32
        ).astype(jnp.bfloat16)
        delta = jnp.sum(g_part.astype(jnp.float32) * attn_out.astype(jnp.float32), axis=-1)
        dprobs = jnp.einsum("nqhd,nkhd->nhqk", g_part, v_part, preferred_element_type=jnp.float32)
        dscore = (probs * (dprobs - jnp.transpose(delta, (0, 2, 1))[..., None]) * scaling).astype(
            jnp.bfloat16
        )
        dq_part = jnp.einsum(
            "nhqk,nkhd->nqhd", dscore, k_part, preferred_element_type=jnp.float32
        ).astype(jnp.bfloat16)
        dk_part = jnp.einsum("nhqk,nqhd->nkhd", dscore, q_part, preferred_element_type=jnp.float32)
        dv_part = jnp.einsum("nhqk,nqhd->nkhd", probs_b, g_part, preferred_element_type=jnp.float32)
        return (dq_part, dk_part, dv_part)

    items = tuple(
        (grouped(array) for array in (q_block, g_block, k_window, v_window, seg_query, seg_key))
    )
    dq_all, dk_window, dv_window = lax.map(one_group, items)
    dq_all = dq_all.reshape(length, head_count, head_width)

    def fold_window(window):
        window = window.reshape((block_count, 2 * DOC, head_count, head_width))
        later = jnp.concatenate([window[1:, :DOC], jnp.zeros_like(window[:1, :DOC])], axis=0)
        return (
            (window[:, DOC:] + later).reshape(length, head_count, head_width).astype(jnp.bfloat16)
        )

    return (dq_all, fold_window(dk_window), fold_window(dv_window))


def on_device(queries, keys, values, grad_out, proj_in, segments):
    per_group = H // KV
    own_rows = queries.shape[1]
    q_split = queries.reshape(1, own_rows, H, HD)
    g_split = grad_out.reshape(1, own_rows, H, HD)
    q_heads, g_heads = side_by_side((q_split, g_split), "seq", 2, 1, 0)
    k_split = jnp.repeat(keys.reshape(1, own_rows, KV, HD), per_group, axis=2)
    v_split = jnp.repeat(values.reshape(1, own_rows, KV, HD), per_group, axis=2)
    k_heads, v_heads = side_by_side((k_split, v_split), "seq", 2, 1, 0)
    dq_all, dk_all, dv_all = attend(q_heads[0], k_heads[0], v_heads[0], g_heads[0], segments[0])
    length = dq_all.shape[0]
    head_count = dq_all.shape[1]
    grad_rows = jnp.concatenate(
        [
            dq_all.reshape(length, head_count * HD),
            jnp.stack([dk_all, dv_all], axis=1).reshape(length, 2 * head_count * HD),
        ],
        axis=1,
    )
    total = jnp.einsum(
        "lr,lc->rc",
        lax.all_gather(proj_in, "seq", axis=1, tiled=True)[0],
        grad_rows,
        preferred_element_type=jnp.float32,
    )
    q_term = total[:, : head_count * HD]
    kv_local = total[:, head_count * HD :].reshape(RANK, 2, head_count, HD)
    global_heads = lax.axis_index("seq") * head_count + jnp.arange(head_count)
    owners = ((global_heads // per_group)[:, None] == jnp.arange(KV)[None, :]).astype(jnp.float32)
    kv_term = jnp.einsum(
        "rshd,hg->rsgd", kv_local, owners, precision=lax.Precision.HIGHEST
    ).reshape(RANK, 2 * KV * HD)
    kv_part = summed_on_arrival(kv_term.astype(jnp.bfloat16), "seq", 1)
    grad_q_proj, grad_kv_proj = tuple(
        (
            part.astype(jnp.float32)
            for part in sum_packed(
                (q_term.astype(jnp.bfloat16), kv_part.astype(jnp.bfloat16)), "dp", (0, 0)
            )
        )
    )
    return (grad_q_proj, grad_kv_proj)


def solution(mesh):
    in_specs = (
        P("dp", "seq", None),
        P("dp", "seq", None),
        P("dp", "seq", None),
        P("dp", "seq", None),
        P("dp", "seq", None),
        P("dp", None),
    )
    out_specs = (P("dp", "seq"), P("dp", "seq"))
    return jax.shard_map(
        on_device, mesh=mesh, in_specs=in_specs, out_specs=out_specs, check_vma=False
    )
```

profile of v0, /device:TPU:4, one launch (start us, length us, event | category | flops | bytes accessed | tf_op | source)
XLA Modules:
  0.0 561.9 jit_solution(7488175196275892081)
XLA Ops:
  9.6 1.5 pad_maximum_fusion
  11.1 16.8 %all-to-all-start = ((bf16[2,128,32,128]{3,1,0,2:T(8,128)(2,1)}), bf16[2,128,32,128]{3,1,0,2:T(8,128)(2,1)S(1)}, u32[]{:S(2)}, u32[]{:S(2)}) async-start(bf16[2,128,32,128]{3,1,0,2:T(8,128)(2,1)} %pad_maximum_fusion), calls=%async_computation | async-start | bytes 4194304 | tf_op jit(solution)/shard_map/all_to_all | solution.py:16
  27.9 1.6 copy.44
  29.6 2.3 copy.45
  31.8 2.9 pad_maximum_fusion.2
  34.7 87.5 %all-to-all-done = bf16[2,128,32,128]{3,1,0,2:T(8,128)(2,1)S(1)} async-done(((bf16[2,128,32,128]{3,1,0,2:T(8,128)(2,1)}), bf16[2,128,32,128]{3,1,0,2:T(8,128)(2,1)S(1)}, u32[]{:S(2)}, u32[]{:S(2)}) %all-to-all-start) | async-done | bytes 2097184 | tf_op jit(solution)/shard_map/all_to_all | solution.py:16
  122.2 7.7 %all-to-all-start.1 = ((bf16[2,128,32,128]{1,3,0,2:T(8,128)(2,1)}), bf16[2,128,32,128]{1,3,0,2:T(8,128)(2,1)}, u32[]{:S(2)}, u32[]{:S(2)}) async-start(bf16[2,128,32,128]{1,3,0,2:T(8,128)(2,1)} %pad_maximum_fusion.2), calls=%async_computation.1 | async-start | bytes 4194304 | tf_op jit(solution)/shard_map/all_to_all | solution.py:16
  132.3 1.4 fusion.77
  133.7 91.0 %all-to-all-done.1 = bf16[2,128,32,128]{1,3,0,2:T(8,128)(2,1)} async-done(((bf16[2,128,32,128]{1,3,0,2:T(8,128)(2,1)}), bf16[2,128,32,128]{1,3,0,2:T(8,128)(2,1)}, u32[]{:S(2)}, u32[]{:S(2)}) %all-to-all-start.1) | async-done | bytes 2097184 | tf_op jit(solution)/shard_map/all_to_all | solution.py:16
  224.8 3.4 fusion.78
  228.1 2.2 pad_maximum_fusion.1
  230.4 87.0 %while.15 = (s32[]{:T(128)}, bf16[8,4,128,1,128]{4,2,1,0,3:T(8,128)(2,1)}, f32[8,4,256,1,128]{4,2,1,0,3:T(8,128)}, f32[8,4,256,1,128]{4,2,1,0,3:T(8,128)}, bf16[...) while((s32[]{:T(128)}, ...), condition=%wide.region_4.5_spmd.clone, body=%wide.region_0.4_spmd.clone.sunk | while | flops 204111616 | bytes 10627197 | solution.py:104
  230.5 2.2 fusion.111
  232.7 1.2 convolution_bitcast_fusion.4
  234.1 1.4 fusion.112
  235.5 1.3 fusion.113
  239.2 1.2 fusion.114
  241.3 2.2 fusion.111
  243.5 1.2 convolution_bitcast_fusion.4
  244.9 1.4 fusion.112
  246.3 1.3 fusion.113
  250.0 1.2 fusion.114
  252.1 2.2 fusion.111
  254.3 1.2 convolution_bitcast_fusion.4
  255.8 1.4 fusion.112
  257.1 1.3 fusion.113
  259.8 1.2 constant_dynamic-update-slice_fusion.6
  261.0 1.2 fusion.114
  263.1 2.2 fusion.111
  265.3 1.2 convolution_bitcast_fusion.4
  266.7 1.4 fusion.112
  268.1 1.3 fusion.113
  271.9 1.2 fusion.114
  274.0 2.2 fusion.111
  276.2 1.2 convolution_bitcast_fusion.4
  277.6 1.4 fusion.112
  279.0 1.3 fusion.113
  282.7 1.2 fusion.114
  284.9 2.2 fusion.111
  287.1 1.2 convolution_bitcast_fusion.4
  288.5 1.4 fusion.112
  289.9 1.3 fusion.113
  293.6 1.2 fusion.114
  295.7 2.2 fusion.111
  297.9 1.2 convolution_bitcast_fusion.4
  299.3 1.4 fusion.112
  300.7 1.3 fusion.113
  304.5 1.2 fusion.114
  306.6 2.2 fusion.111
  308.8 1.2 convolution_bitcast_fusion.4
  310.3 1.4 fusion.112
  311.6 1.3 fusion.113
  315.3 1.2 fusion.114
  317.4 1.9 slice.68
  319.2 1.7 slice.70
  321.3 1.9 copy-done.4
  323.7 2.8 copy.53
  326.5 1.3 copy.54
  327.9 34.8 %all-gather.2.cloned.1.call-done = bf16[1,4096,256]{2,1,0:T(8,128)(2,1)} async-done(((bf16[1,128,256]{2,1,0:T(8,128)(2,1)}), bf16[1,4096,256]{2,1,0:T(8,128)(2,1)}) %all-gather.2.cloned.1.call-update) | async-done | bytes 2097168 | tf_op jit(solution)/shard_map/all_gather | solution.py:138
  362.6 2.9 fusion.62
  366.5 19.4 %all-to-all-start.2 = ((bf16[32,256,32]{1,2,0:T(8,128)(2,1)}), bf16[32,256,32]{1,2,0:T(8,128)(2,1)S(1)}, u32[]{:S(2)}, u32[]{:S(2)}) async-start(bf16[32,256,32]{1,2,0:T(8,128)(2,1)} %bitcast.39), calls=%async_computation.2 | async-start | bytes 1048576 | tf_op jit(solution)/shard_map/all_to_all | solution.py:28
  386.2 17.7 %all-to-all-done.2 = bf16[32,256,32]{1,2,0:T(8,128)(2,1)S(1)} async-done(((bf16[32,256,32]{1,2,0:T(8,128)(2,1)}), bf16[32,256,32]{1,2,0:T(8,128)(2,1)S(1)}, u32[]{:S(2)}, u32[]{:S(2)}) %all-to-all-start.2) | async-done | bytes 524320 | tf_op jit(solution)/shard_map/all_to_all | solution.py:28
  405.0 147.4 %reduce-scatter.2.cloned.1.call-done = bf16[16,128]{1,0:T(8,128)(2,1)} async-done(((bf16[512,128]{1,0:T(8,128)(2,1)}), bf16[16,128]{1,0:T(8,128)(2,1)}) %reduce-scatter.2.cloned.1.call-update) | async-done | bytes 4112 | tf_op jit(solution)/shard_map/reduce_scatter | solution.py:38
  553.8 1.3 slice_convert_fusion.1
  (122 shorter events, 35.7 us)
Async XLA Ops:
  11.1 111.1 %all-to-all-start = ((bf16[2,128,32,128]{3,1,0,2:T(8,128)(2,1)}), bf16[2,128,32,128]{3,1,0,2:T(8,128)(2,1)S(1)}, u32[]{:S(2)}, u32[]{:S(2)}) async-start(bf16[2,128,32,128]{3,1,0,2:T(8,128)(2,1)} %pad_maximum_fusion), calls=%async_computation | async-start | bytes 4194304 | tf_op jit(solution)/shard_map/all_to_all | solution.py:16
  34.7 96.1 %copy-start.7 = (s32[1,4096]{1,0:T(1,128)S(1)}, s32[1,4096]{1,0:T(1,128)}, u32[]{:S(2)}) copy-start(s32[1,4096]{1,0:T(1,128)} %param.13) | copy-start | bytes 49156
  122.2 102.5 %all-to-all-start.1 = ((bf16[2,128,32,128]{1,3,0,2:T(8,128)(2,1)}), bf16[2,128,32,128]{1,3,0,2:T(8,128)(2,1)}, u32[]{:S(2)}, u32[]{:S(2)}) async-start(bf16[2,128,32,128]{1,3,0,2:T(8,128)(2,1)} %pad_maximum_fusion.2), calls=%async_computation.1 | async-start | bytes 4194304 | tf_op jit(solution)/shard_map/all_to_all | solution.py:16
  130.0 232.6 %all-gather.2.cloned.1.call-start = ((), (), s32[]{:S(2)}) async-start(), calls=%async_computation.4 | async-start | bytes 2162688 | tf_op jit(solution)/shard_map/all_gather | solution.py:138
  224.7 3.4 copy-start
  224.8 3.4 copy-start.1
  224.8 3.4 copy-start.2
  317.4 3.6 copy-start.3
  321.0 2.2 copy-start.4
  323.7 2.8 copy-start.6
  326.5 36.1 %copy-start.5 = (bf16[4096,2,1,128]{0,3,1,2:T(8,128)(2,1)S(1)}, bf16[4096,2,1,128]{0,3,1,2:T(8,128)(2,1)}, u32[]{:S(2)}) copy-start(bf16[4096,2,1,128]{0,3,1,2:T(8,128)(2,1)} %copy.53) | copy-start | bytes 6291460
  366.5 37.4 %all-to-all-start.2 = ((bf16[32,256,32]{1,2,0:T(8,128)(2,1)}), bf16[32,256,32]{1,2,0:T(8,128)(2,1)S(1)}, u32[]{:S(2)}, u32[]{:S(2)}) async-start(bf16[32,256,32]{1,2,0:T(8,128)(2,1)} %bitcast.39), calls=%async_computation.2 | async-start | bytes 1048576 | tf_op jit(solution)/shard_map/all_to_all | solution.py:28
  386.0 166.4 %reduce-scatter.2.cloned.1.call-start = ((), (), s32[]{:S(2)}) async-start(), calls=%async_computation.5 | async-start | bytes 135168 | tf_op jit(solution)/shard_map/reduce_scatter | solution.py:38
Sparse Core Ops, SparseCore 0:
  133.5 229.0 all-gather.1
  405.1 147.2 reduce-scatter.1
where the time goes:
time: 564 us; the launch traced here: 562 us
  waiting for transfers between devices  379 us (67%)
  matrix products  70.5 us (12%)
  starting transfers between devices  44.1 us (8%)
  local copies, waits for them, and re-layouts  42.1 us (7%)
  between operations  14.3 us (3%)
  other arithmetic  11.2 us (2%)
    all_to_all x2, waiting for transfers between devices, side_by_side(): lax.all_to_all(both, axis, split_axis=split_dim, concat_axis=concat_dim,...  179 us
    reduce_scatter x1, waiting for transfers between devices, sum_packed(): lax.psum_scatter(lines, axis, tiled=True).reshape(-1)  147 us
    all_gather x1, waiting for transfers between devices, on_device(): lax.all_gather(proj_in, 'seq', axis=1, tiled=True)[0]  34.8 us
    all_to_all x2, starting transfers between devices, side_by_side(): lax.all_to_all(both, axis, split_axis=split_dim, concat_axis=concat_dim,...  24.6 us
    all_to_all x1, starting transfers between devices, summed_on_arrival(): tiles = lax.all_to_all(cut_along(value, dim, size), axis, 0, 0, tiled=True)  19.4 us
    dynamic_update_slice x40, local copies, waits for them, and re-layouts, attend(): dq_all, dk_window, dv_window = lax.map(one_group, items)  18.2 us
    all_to_all x1, waiting for transfers between devices, summed_on_arrival(): tiles = lax.all_to_all(cut_along(value, dim, size), axis, 0, 0, tiled=True)  17.7 us
    sub x8, matrix products, one_group(): probs = jnp.exp(scores - jnp.max(scores, axis=-1, keepdims=True))  17.7 us
  transfers between devices with their start and end apart: 5, of which 5 were waited for; matrix products, arithmetic and copies ran while one was open for 20% of the time, Pallas kernels for 0%

commit v1 on v0

v1 whole, which is shorter than its diff:
```python
import functools
import math

import jax
import jax.numpy as jnp
from jax import lax
from jax.experimental import pallas as pl
from jax.experimental.pallas import tpu as pltpu
from jax.sharding import PartitionSpec as P

MESH = pl.DeviceIdType.MESH
F32 = jnp.float32
BF16 = jnp.bfloat16
B = 128
NEG = -1e30


def nt(a, b):
    return lax.dot_general(a, b, (((1,), (1,)), ((), ())), preferred_element_type=F32)


def tn(a, b):
    return lax.dot_general(a, b, (((0,), (0,)), ((), ())), preferred_element_type=F32)


def nn(a, b):
    return lax.dot_general(a, b, (((1,), (0,)), ((), ())), preferred_element_type=F32)


class Grid:
    def __init__(self, ZH, Y, C, ZL, X):
        self.ZH, self.Y, self.C, self.ZL, self.X = ZH, Y, C, ZL, X
        self.Z = ZH * ZL
        self.G = ZL // 2


REAL = Grid(4, 4, 2, 8, 4)


def kernel(
    gr,
    q_hbm, k_hbm, v_hbm, do_hbm, pj_hbm, seg_hbm,
    out_ref,
    seg_ref,     q_v, do_v, kvw, pjw, pjt, bias, mo, mp, pw, dsw,
    own, csend, crecv, s1, r1, s2, r2, zq, zkv, zsrc, zr,
    ld_sem, kv_sem, pj_sem, sg_sem, hs_sem, hr_sem, cs_sem, cr_sem, s1s_sem, s1r_sem, s2s_sem, s2r_sem, zs_sem, zr_sem, rel_sem,
):
    ZH, Y, ZL, X, Z, G = gr.ZH, gr.Y, gr.ZL, gr.X, gr.Z, gr.G
    HG = 2 * X
    SEQ = ZL * X
    dp, seq = lax.axis_index("dp"), lax.axis_index("seq")
    zh, y, c = dp // (2 * Y), (dp // 2) % Y, dp % 2
    zl, x = seq // X, seq % X
    z = zh * ZL + zl

    def at(zh_, y_, c_, zl_, x_):
        return ((zh_ * Y + y_) * 2 + c_, zl_ * X + x_)

    def along_z(k):
        there = lax.rem(z + k + Z, Z)
        return at(there // ZL, y, c, lax.rem(there, ZL), x)

    def along_y(k):
        return at(zh, lax.rem(y + k, Y), c, zl, x)

    def along_x(k):
        return at(zh, y, c, zl, lax.rem(x + k, X))

    other = at(zh, y, 1 - c, zl, x)
    right = (dp, jnp.minimum(seq + 1, SEQ - 1))
    left = (dp, jnp.maximum(seq - 1, 0))

    def local(src, dst, sem):
        copy = pltpu.make_async_copy(src, dst, sem)
        copy.start()
        return copy

    def remote(src, dst, ssem, rsem, device):
        return pltpu.make_async_remote_copy(src, dst, ssem, rsem, device_id=device, device_id_type=MESH)

    def await_bytes(ref, sem):
        pltpu.make_async_copy(ref, ref, sem).wait()

    seg_in = local(seg_hbm, seg_ref, sg_sem)
    kv_in = []
    for g in range(G):
        cols = pl.ds(g * B, B)
        kv_in.append(local(k_hbm.at[0, :, cols], kvw.at[g, 0, pl.ds(0, B)], kv_sem.at[g, 0]))
        kv_in.append(local(v_hbm.at[0, :, cols], kvw.at[g, 1, pl.ds(0, B)], kv_sem.at[g, 1]))
    pj_in = local(pj_hbm.at[0], pjw.at[0], pj_sem)
    big = []
    for g in range(G):
        cols = pl.ds(g * HG * B, HG * B)
        big.append(
            (
                local(q_hbm.at[0, :, cols], q_v.at[:, cols], ld_sem.at[g, 0]),
                local(do_hbm.at[0, :, cols], do_v.at[:, cols], ld_sem.at[g, 1]),
            )
        )

    barrier = pltpu.get_barrier_semaphore()
    near = [other]
    near += [along_y(k) for k in range(1, Y)]
    near += [along_x(k) for k in range(1, X)]
    near += [along_z(k) for k in (1, -1, 2, -2)]
    for device in near:
        pl.semaphore_signal(barrier, inc=1, device_id=device, device_id_type=MESH)

    @pl.when(seq > 0)
    def _():
        pl.semaphore_signal(barrier, inc=1, device_id=left, device_id_type=MESH)

    seg_in.wait()
    start = pl.multiple_of(seq * B, B)
    start_before = pl.multiple_of(jnp.maximum(seq - 1, 0) * B, B)
    seg_i = jnp.broadcast_to(seg_ref[:, pl.ds(start, B)].astype(F32), (B, B))
    seg_p = jnp.broadcast_to(seg_ref[:, pl.ds(start_before, B)].astype(F32), (B, B))
    seg_p = jnp.where(seq > 0, seg_p, -1.0)
    row = lax.broadcasted_iota(jnp.int32, (B, B), 0)
    lane = lax.broadcasted_iota(jnp.int32, (B, B), 1)
    causal = row <= lane
    same = jnp.where(causal, seg_i.T, seg_p.T) == seg_i
    one_bias = jnp.where(same, 0.0, NEG)
    one_mo = jnp.where(causal, 1.0, 0.0).astype(BF16)
    one_mp = jnp.where(causal, 0.0, 1.0).astype(BF16)
    for half in range(2):
        cols = pl.ds(half * B, B)
        bias[:, cols] = one_bias
        mo[:, cols] = one_mo
        mp[:, cols] = one_mp

    for copy in kv_in:
        copy.wait()
    pj_in.wait()

    @pl.when(seq < SEQ - 1)
    def _():
        pl.semaphore_wait(barrier, len(near) + 1)

    @pl.when(seq == SEQ - 1)
    def _():
        pl.semaphore_wait(barrier, len(near))

    def halo_kv(g):
        return remote(
            kvw.at[g, :, pl.ds(0, B)], kvw.at[g, :, pl.ds(B, B)], hs_sem.at[g], hr_sem.at[g], right
        )

    halo_pj = remote(pjw.at[0], pjw.at[1], hs_sem.at[G], hr_sem.at[G], right)

    @pl.when(seq < SEQ - 1)
    def _():
        halo_kv(0).start()
        halo_pj.start()
        for g in range(1, G):
            halo_kv(g).start()

    @pl.when(seq == 0)
    def _():
        kvw[:, :, B:] = jnp.zeros((G, 2, B, B), BF16)
        pjw[1] = jnp.zeros(pjw.shape[1:], BF16)

    relays = []
    reach = 2
    while reach < Z // 2:
        relays.append(reach)
        reach *= 2

    def relay_out(n):
        for k in (relays[n], -relays[n]):
            pl.semaphore_signal(rel_sem.at[n], inc=1, device_id=along_z(k), device_id_type=MESH)

    def relay_in(n):
        pl.semaphore_wait(rel_sem.at[n], 2)

    relay_out(0)

    first_core = c == 0

    def transposed(n):
        t = pjw[n].astype(F32).T
        mine, theirs = [], []
        for yy in range(Y):
            for hh in range(ZH):
                o = (hh * Y + yy) * 2
                even, odd = t[o * 8 : o * 8 + 8], t[o * 8 + 8 : o * 8 + 16]
                mine.append(jnp.where(first_core, even, odd))
                theirs.append(jnp.where(first_core, odd, even))
        pjt[:, n * B : (n + 1) * B] = jnp.concatenate(mine + theirs, axis=0).astype(BF16)

    transposed(0)
    R = pjt.shape[0] // 2
    YR = R // Y

    scale = B**-0.5
    to_log2 = scale * math.log2(math.e)
    row2 = lax.broadcasted_iota(jnp.int32, (B, 2 * B), 0)
    lane2 = lax.broadcasted_iota(jnp.int32, (B, 2 * B), 1)
    causal2 = row2 <= jnp.bitwise_and(lane2, B - 1)

    def stacked(ref, off, count):
        return jnp.concatenate([ref[:, off + n * B : off + (n + 1) * B] for n in range(count)], axis=0)

    def compute(g):
        base = g * HG * B
        for copy in big[g]:
            copy.wait()

        @pl.when(seq > 0)
        def _():
            halo_kv(g).wait_recv()

        kw, vw = kvw[g, 0], kvw[g, 1]
        for hp in range(HG // 2):
            off = base + hp * 2 * B
            st = nt(kw, stacked(q_v, off, 2))
            dpt = nt(vw, stacked(do_v, off, 2))
            s = jnp.where(causal2, st[:B], st[B:]) * to_log2 + bias[...]
            p = jnp.exp2(s - jnp.max(s, axis=0, keepdims=True))
            p = p * (1.0 / jnp.sum(p, axis=0, keepdims=True))
            d = jnp.where(causal2, dpt[:B], dpt[B:])
            delta = jnp.sum(p * d, axis=0, keepdims=True)
            ds = (p * ((d - delta) * scale)).astype(BF16)
            pb = p.astype(BF16)
            cols = pl.ds(hp * 2 * B, 2 * B)
            pw[:B, cols] = pb * mo[...]
            pw[B:, cols] = pb * mp[...]
            dsw[:B, cols] = ds * mo[...]
            dsw[B:, cols] = ds * mp[...]
        if g == 0:

            @pl.when(seq > 0)
            def _():
                halo_pj.wait_recv()

            transposed(1)
        dqt = tn(kw, dsw[...]).astype(BF16)
        dk = nn(dsw[...], stacked(q_v, base, HG))
        dv = nn(pw[...], stacked(do_v, base, HG))
        for hp in range(HG // 2):
            lo = hp * 2 * B
            pair = jnp.concatenate([dqt[:, lo : lo + B], dqt[:, lo + B : lo + 2 * B]], axis=0)
            gq = nt(pjt[:, :B], pair)
            for n in range(2):
                own[g, 2 * hp + n] = gq[:R, n * B : (n + 1) * B]
                csend[g, 2 * hp + n] = gq[R:, n * B : (n + 1) * B].astype(BF16)
        gkv = nn(pjt[...], jnp.concatenate([dk, dv], axis=1).astype(BF16))
        for n in range(2):
            own[g, HG + n] = gkv[:R, n * B : (n + 1) * B]
            csend[g, HG + n] = gkv[R:, n * B : (n + 1) * B].astype(BF16)

    def core_copy(g):
        return remote(csend.at[g], crecv.at[g], cs_sem.at[g], cr_sem.at[g], other)

    def s1_copy(g, k):
        rows = pl.ds(pl.multiple_of(lax.rem(y + k, Y) * YR, YR), YR)
        return remote(s1.at[g, :, rows], r1.at[g, k - 1], s1s_sem.at[g], s1r_sem.at[g], along_y(k))

    def s2_copy(g, k):
        return remote(s2.at[g, lax.rem(x + k, X)], r2.at[g, k - 1], s2s_sem.at[g], s2r_sem.at[g], along_x(k))

    def step1(g):
        core_copy(g).wait_recv()
        s1[g] = (own[g] + crecv[g].astype(F32)).astype(BF16)
        for k in range(1, Y):
            s1_copy(g, k).start()

    def step2(g):
        await_bytes(r1.at[g], s1r_sem.at[g])
        rows = pl.ds(pl.multiple_of(y * YR, YR), YR)
        total = s1[g, :, rows].astype(F32)
        for k in range(1, Y):
            total = total + r1[g, k - 1].astype(F32)
        total = total.astype(BF16)
        for xx in range(X):
            s2[g, xx, 0] = total[xx]
            s2[g, xx, 1] = total[X + xx]
            s2[g, xx, 2] = total[HG]
            s2[g, xx, 3] = total[HG + 1]
        for k in range(1, X):
            s2_copy(g, k).start()

    def step3(g):
        await_bytes(r2.at[g], s2r_sem.at[g])
        total = s2[g, x].astype(F32)
        for k in range(1, X):
            total = total + r2[g, k - 1].astype(F32)
        zq[2 * g] = total[0]
        zq[2 * g + 1] = total[1]
        zkv[g] = total[2]
        zkv[G + g] = total[3]

    sent = set()

    def z_send(done):
        ready = [n for n in range(ZL) if n // 2 < done and n % G < done and n not in sent]
        sent.update(ready)
        for n in ready:
            for hh in range(ZH):
                rows = pl.ds(hh * 8, 8)
                zsrc[n, hh] = jnp.concatenate([zq[n, rows], zkv[n, rows]], axis=0).astype(BF16)
        for j in sorted(range(ZH), key=lambda j: -min(j, ZH - j)):
            for n in ready:
                zh_to = lax.rem(zh + j, ZH)
                k = lax.rem(zh_to * ZL + n - z + Z, Z)

                @pl.when(k != 0)
                def _():
                    remote(
                        zsrc.at[n, zh_to], zr.at[k - 1], zs_sem, zr_sem, at(zh_to, y, c, n, x)
                    ).start()

    for g in range(G):
        compute(g)
        core_copy(g).start()
        if g < len(relays):
            relay_in(g)
            if g + 1 < len(relays):
                relay_out(g + 1)
        if g >= 1:
            step1(g - 1)
        if g >= 2:
            step2(g - 2)
        if g >= 3:
            step3(g - 3)
    step1(G - 1)
    if G >= 2:
        step2(G - 2)
    if G >= 3:
        step3(G - 3)
        z_send(G - 2)
    if G >= 2:
        step3(G - 2)
        z_send(G - 1)
    step2(G - 1)
    step3(G - 1)
    z_send(G)

    @pl.when(seq < SEQ - 1)
    def _():
        for g in range(G):
            halo_kv(g).wait_send()
        halo_pj.wait_send()

    for g in range(G):
        core_copy(g).wait_send()
        await_bytes(r1.at[g], s1s_sem.at[g])
        await_bytes(r2.at[g], s2s_sem.at[g])
    await_bytes(zr, zs_sem)
    await_bytes(zr, zr_sem)
    total = zsrc[zl, zh].astype(F32)
    for k in range(Z - 1):
        total = total + zr[k].astype(F32)
    out_ref[...] = total


def on_device(gr, queries, keys, values, grad_out, proj_in, segments):
    G, X, Y, ZH, ZL, Z = gr.G, gr.X, gr.Y, gr.ZH, gr.ZL, gr.Z
    HG = 2 * X
    NB = HG + 2
    rank = proj_in.shape[-1]
    R = rank // 2
    YR = R // Y
    hbm = pl.BlockSpec(memory_space=pltpu.HBM)
    vmem = pl.BlockSpec(memory_space=pltpu.VMEM)
    dma = pltpu.SemaphoreType.DMA
    out = pl.pallas_call(
        functools.partial(kernel, gr),
        out_shape=jax.ShapeDtypeStruct((16, B), F32),
        in_specs=[hbm] * 6,
        out_specs=vmem,
        scratch_shapes=[
            pltpu.VMEM(segments.shape, jnp.int32),
            pltpu.VMEM((B, G * HG * B), BF16),
            pltpu.VMEM((B, G * HG * B), BF16),
            pltpu.VMEM((G, 2, 2 * B, B), BF16),
            pltpu.VMEM((2, B, rank), BF16),
            pltpu.VMEM((rank, 2 * B), BF16),
            pltpu.VMEM((B, 2 * B), F32),
            pltpu.VMEM((B, 2 * B), BF16),
            pltpu.VMEM((B, 2 * B), BF16),
            pltpu.VMEM((2 * B, HG * B), BF16),
            pltpu.VMEM((2 * B, HG * B), BF16),
            pltpu.VMEM((G, NB, R, B), F32),
            pltpu.VMEM((G, NB, R, B), BF16),
            pltpu.VMEM((G, NB, R, B), BF16),
            pltpu.VMEM((G, NB, R, B), BF16),
            pltpu.VMEM((G, Y - 1, NB, YR, B), BF16),
            pltpu.VMEM((G, X, 4, YR, B), BF16),
            pltpu.VMEM((G, X - 1, 4, YR, B), BF16),
            pltpu.VMEM((ZL, YR, B), F32),
            pltpu.VMEM((ZL, YR, B), F32),
            pltpu.VMEM((ZL, ZH, 16, B), BF16),
            pltpu.VMEM((Z - 1, 16, B), BF16),
            dma((G, 2)),
            dma((G, 2)),
            dma,
            dma,
            dma((G + 1,)),
            dma((G + 1,)),
            dma((G,)),
            dma((G,)),
            dma((G,)),
            dma((G,)),
            dma((G,)),
            dma((G,)),
            dma,
            dma,
            pltpu.SemaphoreType.REGULAR((4,)),
        ],
        compiler_params=pltpu.CompilerParams(
            collective_id=0, has_side_effects=True, vmem_limit_bytes=64 * 1024 * 1024
        ),
        name="packed_grads",
    )(queries, keys, values, grad_out, proj_in, segments)
    x = lax.axis_index("seq") % X
    width = B // X
    return out[:8], lax.dynamic_slice(out, (8, x * width), (8, width))


def solution(mesh, gr=REAL):
    in_specs = (P("dp", "seq", None),) * 5 + (P("dp", None),)
    out_specs = (P("dp", "seq"), P("dp", "seq"))
    return jax.shard_map(
        functools.partial(on_device, gr), mesh=mesh, in_specs=in_specs, out_specs=out_specs, check_vma=False
    )
```

time: 564 us -> 67.9 us (0.12)
  the two profiles are of different devices: /device:TPU:4 before, /device:TPU:96 now
where the time goes in v1:
time: 67.9 us; the launch traced here: 67.7 us
  Pallas kernels  65 us (96%)
  local copies, waits for them, and re-layouts  2 us (3%)
    pallas_call x1, Pallas kernels, on_device(): pl.pallas_call(functools.partial(kernel, gr), out_shape=jax.ShapeDtypeStr...  65 us
    dynamic_slice x1, local copies, waits for them, and re-layouts, on_device(): return (out[:8], lax.dynamic_slice(out, (8, x * width), (8, width)))  1.4 us

profile of v1, /device:TPU:96, one launch (start us, length us, event | category | flops | bytes accessed | tf_op | source)
XLA Modules:
  0.0 67.7 jit_solution(14432273636610032695)
XLA Ops:
  0.6 65.0 %packed_grads.1 = f32[16,128]{1,0:T(8,128)} custom-call(bf16[1,128,4096]{2,1,0:T(8,128)(2,1)} %q_hbm.1, bf16[1,128,512]{2,1,0:T(8,128)(2,1)} %k_hbm.1, bf16[1,128,512]{2,1,0:T(8,128)(2,1)} %v_hbm.1, bf16[1,128,4096]{2,1,0:T(8,128)(2,1)} %do_hbm.1, bf16[1,128,256]{2,1,0:T(8,128)(2,1)} %pj_hbm.1, s32[1,4096]{1,0:T(1,128)} %seg_hbm.1), custom_call_target="tpu_custom_call" | custom-call | tf_op jit(solution)/shard_map/packed_grads/pallas_call | solution.py:367
  65.7 0.0 copy-start
  65.7 1.4 %constant_dynamic-slice_fusion = f32[8,32]{1,0:T(8,128)} fusion(f32[16,128]{1,0:T(8,128)} %packed_grads.1, s32[]{:T(128)S(6)} %select_n.11), kind=kLoop, calls=%fused_computation | loop fusion | bytes 2052 | tf_op jit(solution)/shard_map/dynamic_slice | solution.py:418
  67.1 0.0 copy-done
  67.1 0.6 slice.3
Async XLA Ops:
  65.7 1.4 %copy-start = (f32[16,128]{1,0:T(8,128)S(1)}, f32[16,128]{1,0:T(8,128)}, u32[]{:S(2)}) copy-start(f32[16,128]{1,0:T(8,128)} %packed_grads.1) | copy-start | bytes 24580

commit v2 on v1

--- a/solution.py
+++ b/solution.py
@@ -42,8 +42,9 @@
     q_hbm, k_hbm, v_hbm, do_hbm, pj_hbm, seg_hbm,
     out_ref,
     seg_ref,     q_v, do_v, kvw, pjw, pjt, bias, mo, mp, pw, dsw,
-    own, csend, crecv, s1, r1, s2, r2, zq, zkv, zsrc, zr,
-    ld_sem, kv_sem, pj_sem, sg_sem, hs_sem, hr_sem, cs_sem, cr_sem, s1s_sem, s1r_sem, s2s_sem, s2r_sem, zs_sem, zr_sem, rel_sem,
+    own, csend, crecv, zq, zkv, zsrc, zr,
+    ax0, ax1, ay0, ay1, by0, by1, bx0, bx1,
+    ld_sem, kv_sem, pj_sem, sg_sem, hs_sem, hr_sem, cs_sem, cr_sem, ax_sem, ay_sem, by_sem, bx_sem, zs_sem, zr_sem, rel_sem,
 ):
     ZH, Y, ZL, X, Z, G = gr.ZH, gr.Y, gr.ZL, gr.X, gr.Z, gr.G
     HG = 2 * X
@@ -61,10 +62,10 @@
         return at(there // ZL, y, c, lax.rem(there, ZL), x)
 
     def along_y(k):
-        return at(zh, lax.rem(y + k, Y), c, zl, x)
+        return at(zh, lax.rem(y + k + Y, Y), c, zl, x)
 
     def along_x(k):
-        return at(zh, y, c, zl, lax.rem(x + k, X))
+        return at(zh, y, c, zl, lax.rem(x + k + X, X))
 
     other = at(zh, y, 1 - c, zl, x)
     right = (dp, jnp.minimum(seq + 1, SEQ - 1))
@@ -100,9 +101,7 @@
 
     barrier = pltpu.get_barrier_semaphore()
     near = [other]
-    near += [along_y(k) for k in range(1, Y)]
-    near += [along_x(k) for k in range(1, X)]
-    near += [along_z(k) for k in (1, -1, 2, -2)]
+    near += [along(k) for along in (along_x, along_y, along_z) for k in (1, -1)]
     for device in near:
         pl.semaphore_signal(barrier, inc=1, device_id=device, device_id_type=MESH)
 
@@ -161,17 +160,19 @@
         pjw[1] = jnp.zeros(pjw.shape[1:], BF16)
 
     relays = []
-    reach = 2
+    reach = 1
     while reach < Z // 2:
         relays.append(reach)
         reach *= 2
 
     def relay_out(n):
-        for k in (relays[n], -relays[n]):
-            pl.semaphore_signal(rel_sem.at[n], inc=1, device_id=along_z(k), device_id_type=MESH)
+        ways = (along_z, along_x, along_y) if n == 0 else (along_z,)
+        for along in ways:
+            for k in (relays[n], -relays[n]):
+                pl.semaphore_signal(rel_sem.at[n], inc=1, device_id=along(k), device_id_type=MESH)
 
     def relay_in(n):
-        pl.semaphore_wait(rel_sem.at[n], 2)
+        pl.semaphore_wait(rel_sem.at[n], 6 if n == 0 else 2)
 
     relay_out(0)
 
@@ -205,6 +206,9 @@
         base = g * HG * B
         for copy in big[g]:
             copy.wait()
+        if g == 0:
+            relay_in(0)
+            relay_out(1)
 
         @pl.when(seq > 0)
         def _():
@@ -234,6 +238,14 @@
                 halo_pj.wait_recv()
 
             transposed(1)
+        else:
+            step0(g - 1)
+        if g == 1:
+            relay_in(1)
+            relay_out(2)
+        if g == 3:
+            relay_in(2)
+            relay_out(3)
         dqt = tn(kw, dsw[...]).astype(BF16)
         dk = nn(dsw[...], stacked(q_v, base, HG))
         dv = nn(pw[...], stacked(do_v, base, HG))
@@ -252,56 +264,79 @@
     def core_copy(g):
         return remote(csend.at[g], crecv.at[g], cs_sem.at[g], cr_sem.at[g], other)
 
-    def s1_copy(g, k):
-        rows = pl.ds(pl.multiple_of(lax.rem(y + k, Y) * YR, YR), YR)
-        return remote(s1.at[g, :, rows], r1.at[g, k - 1], s1s_sem.at[g], s1r_sem.at[g], along_y(k))
-
-    def s2_copy(g, k):
-        return remote(s2.at[g, lax.rem(x + k, X)], r2.at[g, k - 1], s2s_sem.at[g], s2r_sem.at[g], along_x(k))
+    class Exchange:
+        def __init__(self, place, along, blocks, got, sem):
+            self.place, self.along, self.blocks, self.got, self.sem = place, along, blocks, got, sem
+
+        def start(self, g):
+            for k in (2, 1, 3):
+                remote(
+                    self.blocks.at[g, lax.rem(self.place + k, 4)],
+                    self.got.at[g, k - 1],
+                    self.sem.at[g, 0],
+                    self.sem.at[g, 1],
+                    self.along(k),
+                ).start()
+
+        def total(self, g):
+            await_bytes(self.got.at[g], self.sem.at[g, 1])
+            total = self.blocks[g, self.place].astype(F32)
+            for n in range(3):
+                total = total + self.got[g, n].astype(F32)
+            return total
+
+        def sent(self, g):
+            await_bytes(self.got.at[g], self.sem.at[g, 0])
+
+    on_ax = Exchange(x, along_x, ax0, ax1, ax_sem)
+    on_ay = Exchange(y, along_y, ay0, ay1, ay_sem)
+    on_by = Exchange(y, along_y, by0, by1, by_sem)
+    on_bx = Exchange(x, along_x, bx0, bx1, bx_sem)
+
+    def step0(g):
+        core_copy(g).wait_recv()
+        for n in range(X):
+            ax0[g, n] = (own[g, X + n] + crecv[g, X + n].astype(F32)).astype(BF16)
+        on_ax.start(g)
+        for at_, b in enumerate([*range(X), HG, HG + 1]):
+            both = (own[g, b] + crecv[g, b].astype(F32)).astype(BF16)
+            for n in range(Y):
+                by0[g, n, at_ * YR : (at_ + 1) * YR] = both[n * YR : (n + 1) * YR]
+        on_by.start(g)
 
     def step1(g):
-        core_copy(g).wait_recv()
-        s1[g] = (own[g] + crecv[g].astype(F32)).astype(BF16)
-        for k in range(1, Y):
-            s1_copy(g, k).start()
+        total = on_ax.total(g).astype(BF16)
+        for n in range(Y):
+            ay0[g, n] = total[n * YR : (n + 1) * YR]
+        on_ay.start(g)
+        total = on_by.total(g).astype(BF16)
+        for n in range(X):
+            bx0[g, n, :YR] = total[n * YR : (n + 1) * YR]
+            bx0[g, n, YR:] = total[X * YR :]
+        on_bx.start(g)
 
     def step2(g):
-        await_bytes(r1.at[g], s1r_sem.at[g])
-        rows = pl.ds(pl.multiple_of(y * YR, YR), YR)
-        total = s1[g, :, rows].astype(F32)
-        for k in range(1, Y):
-            total = total + r1[g, k - 1].astype(F32)
-        total = total.astype(BF16)
-        for xx in range(X):
-            s2[g, xx, 0] = total[xx]
-            s2[g, xx, 1] = total[X + xx]
-            s2[g, xx, 2] = total[HG]
-            s2[g, xx, 3] = total[HG + 1]
-        for k in range(1, X):
-            s2_copy(g, k).start()
-
-    def step3(g):
-        await_bytes(r2.at[g], s2r_sem.at[g])
-        total = s2[g, x].astype(F32)
-        for k in range(1, X):
-            total = total + r2[g, k - 1].astype(F32)
-        zq[2 * g] = total[0]
-        zq[2 * g + 1] = total[1]
-        zkv[g] = total[2]
-        zkv[G + g] = total[3]
-
-    sent = set()
-
-    def z_send(done):
-        ready = [n for n in range(ZL) if n // 2 < done and n % G < done and n not in sent]
-        sent.update(ready)
+        zq[2 * g + 1] = on_ay.total(g)
+        total = on_bx.total(g)
+        zq[2 * g] = total[:YR]
+        zkv[g] = total[YR : 2 * YR]
+        zkv[G + g] = total[2 * YR :]
+
+    built, sent = set(), set()
+
+    def z_send(done, parts):
+        ready = [n for n in range(ZL) if n // 2 < done and n % G < done]
         for n in ready:
-            for hh in range(ZH):
-                rows = pl.ds(hh * 8, 8)
-                zsrc[n, hh] = jnp.concatenate([zq[n, rows], zkv[n, rows]], axis=0).astype(BF16)
-        for j in sorted(range(ZH), key=lambda j: -min(j, ZH - j)):
+            if n not in built:
+                built.add(n)
+                for hh in range(ZH):
+                    rows = pl.ds(hh * 8, 8)
+                    zsrc[n, hh] = jnp.concatenate([zq[n, rows], zkv[n, rows]], axis=0).astype(BF16)
+        for zh_to in parts:
             for n in ready:
-                zh_to = lax.rem(zh + j, ZH)
+                if (n, zh_to) in sent:
+                    continue
+                sent.add((n, zh_to))
                 k = lax.rem(zh_to * ZL + n - z + Z, Z)
 
                 @pl.when(k != 0)
@@ -313,28 +348,19 @@
     for g in range(G):
         compute(g)
         core_copy(g).start()
-        if g < len(relays):
-            relay_in(g)
-            if g + 1 < len(relays):
-                relay_out(g + 1)
-        if g >= 1:
-            step1(g - 1)
-        if g >= 2:
-            step2(g - 2)
-        if g >= 3:
-            step3(g - 3)
-    step1(G - 1)
-    if G >= 2:
-        step2(G - 2)
-    if G >= 3:
-        step3(G - 3)
-        z_send(G - 2)
-    if G >= 2:
-        step3(G - 2)
-        z_send(G - 1)
-    step2(G - 1)
-    step3(G - 1)
-    z_send(G)
+    step1(0)
+    step0(3)
+    step1(1)
+    step1(2)
+    step2(0)
+    step1(3)
+    step2(1)
+    relay_in(3)
+    z_send(2, (0, 1, 2))
+    step2(2)
+    z_send(3, (0, 1))
+    step2(3)
+    z_send(4, (0, 1, 2, 3))
 
     @pl.when(seq < SEQ - 1)
     def _():
@@ -344,8 +370,8 @@
 
     for g in range(G):
         core_copy(g).wait_send()
-        await_bytes(r1.at[g], s1s_sem.at[g])
-        await_bytes(r2.at[g], s2s_sem.at[g])
+        for ring in (on_ax, on_ay, on_by, on_bx):
+            ring.sent(g)
     await_bytes(zr, zs_sem)
     await_bytes(zr, zr_sem)
     total = zsrc[zl, zh].astype(F32)
@@ -364,6 +390,10 @@
     hbm = pl.BlockSpec(memory_space=pltpu.HBM)
     vmem = pl.BlockSpec(memory_space=pltpu.VMEM)
     dma = pltpu.SemaphoreType.DMA
+
+    def exchange(rows):
+        return [pltpu.VMEM((G, 4, rows, B), BF16), pltpu.VMEM((G, 3, rows, B), BF16)]
+
     out = pl.pallas_call(
         functools.partial(kernel, gr),
         out_shape=jax.ShapeDtypeStruct((16, B), F32),
@@ -384,14 +414,14 @@
             pltpu.VMEM((G, NB, R, B), F32),
             pltpu.VMEM((G, NB, R, B), BF16),
             pltpu.VMEM((G, NB, R, B), BF16),
-            pltpu.VMEM((G, NB, R, B), BF16),
-            pltpu.VMEM((G, Y - 1, NB, YR, B), BF16),
-            pltpu.VMEM((G, X, 4, YR, B), BF16),
-            pltpu.VMEM((G, X - 1, 4, YR, B), BF16),
             pltpu.VMEM((ZL, YR, B), F32),
             pltpu.VMEM((ZL, YR, B), F32),
             pltpu.VMEM((ZL, ZH, 16, B), BF16),
             pltpu.VMEM((Z - 1, 16, B), BF16),
+            *exchange(R),
+            *exchange(YR),
+            *exchange((X + 2) * YR),
+            *exchange(3 * YR),
             dma((G, 2)),
             dma((G, 2)),
             dma,
@@ -400,10 +430,10 @@
             dma((G + 1,)),
             dma((G,)),
             dma((G,)),
-            dma((G,)),
-            dma((G,)),
-            dma((G,)),
-            dma((G,)),
+            dma((G, 2)),
+            dma((G, 2)),
+            dma((G, 2)),
+            dma((G, 2)),
             dma,
             dma,
             pltpu.SemaphoreType.REGULAR((4,)),

time: 67.9 us -> 63.4 us (0.934)
  the two profiles are of different devices: /device:TPU:96 before, /device:TPU:98 now
where the time goes in v2:
time: 63.4 us; the launch traced here: 63.2 us
  Pallas kernels  60.6 us (96%)
  local copies, waits for them, and re-layouts  2 us (3%)
  between operations  0.67 us (1%)
    pallas_call x1, Pallas kernels, on_device(): pl.pallas_call(functools.partial(kernel, gr), out_shape=jax.ShapeDtypeStr...  60.6 us
    dynamic_slice x1, local copies, waits for them, and re-layouts, on_device(): return (out[:8], lax.dynamic_slice(out, (8, x * width), (8, width)))  1.4 us

profile of v2, /device:TPU:98, one launch (start us, length us, event | category | flops | bytes accessed | tf_op | source)
XLA Modules:
  0.0 63.2 jit_solution(10960937601691792462)
XLA Ops:
  0.6 60.6 %packed_grads.1 = f32[16,128]{1,0:T(8,128)} custom-call(bf16[1,128,4096]{2,1,0:T(8,128)(2,1)} %q_hbm.1, bf16[1,128,512]{2,1,0:T(8,128)(2,1)} %k_hbm.1, bf16[1,128,512]{2,1,0:T(8,128)(2,1)} %v_hbm.1, bf16[1,128,4096]{2,1,0:T(8,128)(2,1)} %do_hbm.1, bf16[1,128,256]{2,1,0:T(8,128)(2,1)} %pj_hbm.1, s32[1,4096]{1,0:T(1,128)} %seg_hbm.1), custom_call_target="tpu_custom_call" | custom-call | tf_op jit(solution)/shard_map/packed_grads/pallas_call | solution.py:397
  61.2 0.0 copy-start
  61.2 1.4 %constant_dynamic-slice_fusion = f32[8,32]{1,0:T(8,128)} fusion(f32[16,128]{1,0:T(8,128)} %packed_grads.1, s32[]{:T(128)S(6)} %select_n.11), kind=kLoop, calls=%fused_computation | loop fusion | bytes 2052 | tf_op jit(solution)/shard_map/dynamic_slice | solution.py:448
  62.6 0.0 copy-done
  62.6 0.6 slice.3
Async XLA Ops:
  61.2 1.4 %copy-start = (f32[16,128]{1,0:T(8,128)S(1)}, f32[16,128]{1,0:T(8,128)}, u32[]{:S(2)}) copy-start(f32[16,128]{1,0:T(8,128)} %packed_grads.1) | copy-start | bytes 24580

commit v3 on v2

--- a/solution.py
+++ b/solution.py
@@ -82,6 +82,16 @@
     def await_bytes(ref, sem):
         pltpu.make_async_copy(ref, ref, sem).wait()
 
+    barrier = pltpu.get_barrier_semaphore()
+    near = [other]
+    near += [along(k) for along in (along_x, along_y, along_z) for k in (1, -1)]
+    for device in near:
+        pl.semaphore_signal(barrier, inc=1, device_id=device, device_id_type=MESH)
+
+    @pl.when(seq > 0)
+    def _():
+        pl.semaphore_signal(barrier, inc=1, device_id=left, device_id_type=MESH)
+
     seg_in = local(seg_hbm, seg_ref, sg_sem)
     kv_in = []
     for g in range(G):
@@ -98,16 +108,6 @@
                 local(do_hbm.at[0, :, cols], do_v.at[:, cols], ld_sem.at[g, 1]),
             )
         )
-
-    barrier = pltpu.get_barrier_semaphore()
-    near = [other]
-    near += [along(k) for along in (along_x, along_y, along_z) for k in (1, -1)]
-    for device in near:
-        pl.semaphore_signal(barrier, inc=1, device_id=device, device_id_type=MESH)
-
-    @pl.when(seq > 0)
-    def _():
-        pl.semaphore_signal(barrier, inc=1, device_id=left, device_id_type=MESH)
 
     seg_in.wait()
     start = pl.multiple_of(seq * B, B)
@@ -378,6 +378,16 @@
     for k in range(Z - 1):
         total = total + zr[k].astype(F32)
     out_ref[...] = total
+
+
+def split(X, total_ref, q_ref, kv_ref):
+    x = lax.axis_index("seq") % X
+    width = B // X
+    q_ref[...] = total_ref[:8]
+    kv = total_ref[8:, :width]
+    for n in range(1, X):
+        kv = jnp.where(x == n, total_ref[8:, n * width : (n + 1) * width], kv)
+    kv_ref[...] = kv
 
 
 def on_device(gr, queries, keys, values, grad_out, proj_in, segments):
@@ -443,9 +453,13 @@
         ),
         name="packed_grads",
     )(queries, keys, values, grad_out, proj_in, segments)
-    x = lax.axis_index("seq") % X
-    width = B // X
-    return out[:8], lax.dynamic_slice(out, (8, x * width), (8, width))
+    return pl.pallas_call(
+        functools.partial(split, X),
+        out_shape=(jax.ShapeDtypeStruct((8, B), F32), jax.ShapeDtypeStruct((8, B // X), F32)),
+        in_specs=[vmem],
+        out_specs=(vmem, vmem),
+        name="split",
+    )(out)
 
 
 def solution(mesh, gr=REAL):

time: 63.4 us -> 63.1 us (level)
  local copies, waits for them, and re-layouts: 2 us -> 0 us
  Pallas kernels: 60.6 us -> 62.3 us
    pallas_call x0 -> x1, Pallas kernels: none -> 1.56 us  [on_device(): pl.pallas_call(functools.partial(split, X), out_shape=(jax.ShapeDtypeStru...]
    dynamic_slice x1 -> x0, local copies, waits for them, and re-layouts: 1.4 us -> none  [on_device(): return (out[:8], lax.dynamic_slice(out, (8, x * width), (8, width)))]
where the time goes in v3:
time: 63.1 us; the launch traced here: 62.9 us
  Pallas kernels  62.3 us (99%)
  between operations  0.64 us (1%)
    pallas_call x1, Pallas kernels, on_device(): pl.pallas_call(functools.partial(kernel, gr), out_shape=jax.ShapeDtypeStr...  60.7 us
    pallas_call x1, Pallas kernels, on_device(): pl.pallas_call(functools.partial(split, X), out_shape=(jax.ShapeDtypeStru...  1.56 us

profile of v3, /device:TPU:98, one launch (start us, length us, event | category | flops | bytes accessed | tf_op | source)
XLA Modules:
  0.0 62.9 jit_solution(1670333093424057459)
XLA Ops:
  0.6 60.7 %packed_grads.1.total_ref = f32[16,128]{1,0:T(8,128)} custom-call(bf16[1,128,4096]{2,1,0:T(8,128)(2,1)} %q_hbm.1, bf16[1,128,512]{2,1,0:T(8,128)(2,1)} %k_hbm.1, bf16[1,128,512]{2,1,0:T(8,128)(2,1)} %v_hbm.1, bf16[1,128,4096]{2,1,0:T(8,128)(2,1)} %do_hbm.1, bf16[1,128,256]{2,1,0:T(8,128)(2,1)} %pj_hbm.1, s32[1,4096]{1,0:T(1,128)} %seg_hbm.1), custom_call_target="tpu_custom_call" | custom-call | tf_op jit(solution)/shard_map/packed_grads/pallas_call | solution.py:407
  61.4 1.6 %split.1 = (f32[8,128]{1,0:T(8,128)}, f32[8,32]{1,0:T(8,128)}) custom-call(f32[16,128]{1,0:T(8,128)} %packed_grads.1.total_ref), custom_call_target="tpu_custom_call" | custom-call | tf_op jit(solution)/shard_map/split/pallas_call | solution.py:456
